TPU v7x, 32 devices: a whole 2x2x4 slice. The times are simulated.
32 devices in a mesh: groups: 2 (over x), layer: 8 (over z, y), ex: 2 (over core).
Axes of the slice: x: 2, y: 2, z: 4, core: 2. Of those that a mesh axis runs over, the one named last changes fastest.
Arguments:
- query_grads: bfloat16 [128, 8, 4096], P(('groups', 'layer')), parts along dimension 0, may hold values from -9000 to 9000
- inv_in: bfloat16 [8, 64, 64], P('layer'), may hold values from -0.4 to 3, as said below
- inv_out: bfloat16 [8, 64, 64], P('layer'), may hold values from -0.4 to 3, as said below
- train_grads: bfloat16 [8, 6144, 4096], P('layer', ('groups', 'ex')), parts along dimension 1, may hold values from -6 to 6
Outputs:
- scores: float32 [64, 6144], P('layer', ('groups', 'ex')), parts along dimension 1
There are 2 independent parts, one for each index of `groups`. A program takes and returns all parts, laid end to end along the dimension named above; an argument that names none is the same for every part. Nothing has to cross between parts.
Inputs may be any that keep to these rules, and one draw needn't show every extreme that they name: `inv_in`: each matrix is symmetric positive definite. `inv_out`: each matrix is symmetric positive definite.
All inputs are finite; a program needn't handle non-finite values.
Results may differ from a plain program's by a relative error of at most 0.0042.
Values may be sent and summed in bfloat16 or wider, within the bound.
A program may use at most 64 MiB of HBM per device.

v0:
```python
import jax
import jax.numpy as jnp
from jax import lax
from jax.sharding import PartitionSpec as P

epsilon = 1e-06


def condition(gradients, left_factor, right_factor):
    picked, modules, length = gradients.shape
    inner_dim = left_factor.shape[-1]
    outer_dim = right_factor.shape[-1]
    shaped = gradients.reshape(picked, modules, inner_dim, outer_dim)
    mixed_rows = jnp.einsum(
        "mij,rmjk->rmik", left_factor, shaped, preferred_element_type=jnp.float32
    ).astype(jnp.bfloat16)
    result = jnp.einsum(
        "rmik,mkl->rmil", mixed_rows, right_factor, preferred_element_type=jnp.float32
    ).astype(jnp.bfloat16)
    return result.reshape(picked, modules, length)


def square_sum(values, axes):
    widened = values.astype(jnp.float32)
    return jnp.sum(widened * widened, axis=axes)


def per_device(query_grads, inv_in, inv_out, train_grads):
    own_rows = query_grads.shape[0]
    arrived = lax.all_to_all(query_grads, "layer", split_axis=1, concat_axis=0, tiled=True)
    conditioned = condition(arrived, inv_in, inv_out)[:, 0]
    resident = train_grads[0]
    totals = lax.psum(square_sum(conditioned, (1,)), "layer")
    own_norm = lax.dynamic_slice_in_dim(totals, lax.axis_index("layer") * own_rows, own_rows, 0)
    reduced = lax.psum_scatter(
        (
            conditioned,
            lax.dot_general(
                conditioned, resident, (((1,), (1,)), ((), ())), preferred_element_type=jnp.float32
            ),
        )[1],
        "layer",
        scatter_dimension=0,
        tiled=True,
    )
    return reduced / jnp.sqrt(own_norm + epsilon)[:, None]


def solution(mesh):
    return jax.shard_map(
        per_device,
        mesh=mesh,
        in_specs=(
            P(("groups", "layer"), None, None),
            P("layer", None, None),
            P("layer", None, None),
            P("layer", ("groups", "ex"), None),
        ),
        out_specs=P("layer", ("groups", "ex")),
        check_vma=False,
    )
```

profile of v0, /device:TPU:0, one launch (start us, length us, event | category | flops | bytes accessed | tf_op | source)
XLA Modules:
  0.0 111.6 jit_solution(4510104877535654839)
XLA Ops:
  6.5 0.0 copy-start
  6.5 0.0 reduce-scatter.2.cloned.1.call-start
  6.5 1.3 %copy.9 = bf16[8,8,4096]{2,0,1:T(8,128)(2,1)S(1)} copy(bf16[8,8,4096]{2,1,0:T(8,128)(2,1)} %param.4) | data formatting | bytes 1048576 | tf_op args[0]
  7.9 21.6 %all_to_all.15 = bf16[8,8,4096]{2,0,1:T(8,128)(2,1)S(1)} all-to-all(bf16[8,8,4096]{2,0,1:T(8,128)(2,1)S(1)} %copy.9), channel_id=1, replica_groups=mesh['groups'=2,'layer'=8,'ex'=2] {'layer'}, dimensions={1} | all-to-all | bytes 1048576 | tf_op jit(solution)/shard_map/all_to_all | solution.py:30
  29.5 1.1 %reshape.20 = bf16[64,64,64]{2,1,0:T(8,128)(2,1)S(1)} reshape(bf16[8,8,1,4096]{3,1,0,2:T(8,128)(2,1)S(1)} %bitcast.47) | data formatting | bytes 1048576 | tf_op jit(solution)/shard_map/reshape.2
  30.6 0.0 copy-done
  30.6 2.0 %multiply_reduce_fusion = (f32[64]{0:T(128)S(1)}, bf16[64,1,64,64]{3,2,0,1:T(8,128)(2,1)S(1)}) fusion(bf16[1,64,64]{2,1,0:T(8,128)(2,1)S(1)} %copy-done, bf16[64,64,64]{2,1,0:T(8,128)(2,1)S(1)} %reshape.20, bf16[1,64,64]{2,1,0:T(8,128)(2,1)} %param.5), kind=kOutput, calls=%fused_computation.2 | convolution fusion | flops 68419520 | bytes 1065216 | tf_op jit(solution)/shard_map/rmik,mkl->rmil/dot_general | solution.py:17
  32.6 0.8 squeeze_reshape.3
  33.4 9.2 %fusion = f32[64,1536]{1,0:T(8,128)} fusion(bf16[64,4096]{1,0:T(8,128)(2,1)S(1)} %squeeze_reshape.3, bf16[1,1536,4096]{2,1,0:T(8,128)(2,1)} %param.7), kind=kOutput, calls=%fused_computation | convolution fusion | flops 805306368 | bytes 13500416 | tf_op jit(solution)/shard_map/dot_general | solution.py:38
  42.7 0.0 reduce-scatter.2.cloned.1.call-update
  42.7 19.6 %psum.7 = f32[64]{0:T(128)S(1)} all-reduce(f32[64]{0:T(128)S(1)} %get-tuple-element.5), channel_id=1, replica_groups=mesh['groups'=2,'layer'=8,'ex'=2] {'layer'}, use_global_device_ids=true, to_apply=%region_2.0 | all-reduce | flops 64 | bytes 512 | tf_op jit(solution)/shard_map/psum | solution.py:33
  62.3 0.1 add_sqrt_fusion
  62.4 40.9 %reduce-scatter.2.cloned.1.call-done = f32[8,1536]{1,0:T(8,128)} async-done(((f32[64,1536]{1,0:T(8,128)}), f32[8,1536]{1,0:T(8,128)}) %reduce-scatter.2.cloned.1.call-update) | async-done | bytes 49168 | tf_op jit(solution)/shard_map/reduce_scatter | solution.py:35
  103.2 1.5 %broadcast_divide_fusion = f32[8,1536]{1,0:T(8,128)} fusion(f32[8,1536]{1,0:T(8,128)} %reduce-scatter.2.cloned.1.call-done, f32[8]{0:T(128)S(1)} %add_sqrt_fusion), kind=kLoop, calls=%fused_computation.7 | loop fusion | flops 12288 | bytes 98336 | tf_op jit(solution)/shard_map/div | solution.py:46
Async XLA Ops:
  6.5 24.1 %copy-start = (bf16[1,64,64]{2,1,0:T(8,128)(2,1)S(1)}, bf16[1,64,64]{2,1,0:T(8,128)(2,1)}, u32[]{:S(2)}) copy-start(bf16[1,64,64]{2,1,0:T(8,128)(2,1)} %param.6) | copy-start | bytes 24580
  6.5 96.7 %reduce-scatter.2.cloned.1.call-start = ((), (), s32[]{:S(2)}) async-start(), calls=%async_computation.2 | async-start | bytes 442368 | tf_op jit(solution)/shard_map/reduce_scatter | solution.py:35
Sparse Core Ops, SparseCore 0:
  42.8 60.3 reduce-scatter.1
where the time goes:
time: 112 us
  blocking collectives  41.2 us (37%)
  waiting for transfers between devices  40.9 us (37%)
  between operations  13.4 us (12%)
  matrix products  11.2 us (10%)
  local copies, waits for them, and re-layouts  3.29 us (3%)
  other arithmetic  1.58 us (1%)
    reduce_scatter x1, waiting for transfers between devices, per_device(): lax.psum_scatter((conditioned, lax.dot_general(conditioned, resident, (((...  40.9 us
    all_to_all x1, blocking collectives, per_device(): lax.all_to_all(query_grads, 'layer', split_axis=1, concat_axis=0, tiled=T...  21.6 us
    psum x1, blocking collectives, per_device(): totals = lax.psum(square_sum(conditioned, (1,)), 'layer')  19.6 us
    dot_general x1, matrix products, per_device(): lax.dot_general(conditioned, resident, (((1,), (1,)), ((), ())), preferre...  9.24 us
  transfers between devices with their start and end apart: 1, of which 1 were waited for; matrix products, arithmetic and copies ran while one was open for 0% of the time, Pallas kernels for 0%

commit v1 on v0

v1 whole, which is shorter than its diff:
```python
import math

import jax
import jax.numpy as jnp
from jax import lax
from jax.experimental import pallas as pl
from jax.experimental.pallas import tpu as pltpu
from jax.sharding import PartitionSpec as P

epsilon = 1e-06
LANES = 128
CHUNK = 16
BLOCKS = 2
MESH = pl.DeviceIdType.MESH
F32 = jnp.float32
BF16 = jnp.bfloat16


def iota(shape, dim):
    return lax.broadcasted_iota(jnp.int32, shape, dim)


def dot(a, b):
    return jnp.dot(a, b, preferred_element_type=F32)


def dot_nt(a, b):
    return lax.dot_general(a, b, (((1,), (1,)), ((), ())), preferred_element_type=F32)


def stack(pieces, axis=0):
    return pieces[0] if len(pieces) == 1 else jnp.concatenate(pieces, axis=axis)


def left_weights(factor):
    size = factor.shape[0]
    half = size // 2
    row, col = iota((size, size), 0), iota((size, size), 1)
    low = row < half
    even_first = jnp.where(low, 2 * row, 2 * (row - half) + 1)
    odd_first = jnp.where(low, 2 * row + 1, 2 * (row - half))
    order = (col == even_first).astype(F32).astype(BF16)
    swapped = (col == odd_first).astype(F32).astype(BF16)
    rows = dot(order, factor).astype(BF16)
    return jnp.where(low, dot_nt(rows, order), dot_nt(rows, swapped)).astype(BF16)


def right_weights(factor):
    size = factor.shape[0]
    row, col = iota((2 * size, size), 0), iota((2 * size, size), 1)
    spread = ((row == col) | (row == col + size)).astype(F32).astype(BF16)
    tiled = dot_nt(dot(spread, factor).astype(BF16), spread)
    row, col = iota((2 * size, 2 * size), 0), iota((2 * size, 2 * size), 1)
    return jnp.where((row < size) == (col < size), tiled, 0.0).astype(BF16)


def kernel(
    layers, own, dims,
    query_hbm, left_hbm, right_hbm, train_hbm,
    out_ref,
    query_v, left_v, right_v, train_v, wide, slabs, arrived, plain, cond, scores, sent, got, norm_sent, norm_got,
    local_sem, train_sem, q_send, q_recv, c_send, c_recv, s_send, s_recv, n_send, n_recv,
):
    groups, slots, per_chunk, chunks, rows_all, block, fold, width, slab_rows = dims
    me = lax.axis_index("layer")
    core = lax.axis_index("ex")

    loads = [
        pltpu.make_async_copy(query_hbm, query_v, local_sem.at[0]),
        pltpu.make_async_copy(left_hbm, left_v, local_sem.at[1]),
        pltpu.make_async_copy(right_hbm, right_v, local_sem.at[2]),
    ]
    for load in loads:
        load.start()
    train_loads = [
        pltpu.make_async_copy(train_hbm.at[pl.ds(b * block, block)], train_v.at[b], train_sem.at[b])
        for b in range(BLOCKS)
    ]

    barrier = pltpu.get_barrier_semaphore()
    for k in range(1, layers):
        pl.semaphore_signal(
            barrier, inc=1, device_id={"layer": lax.rem(me + k, layers)}, device_id_type=MESH
        )
    pl.semaphore_signal(barrier, inc=1, device_id={"ex": 1 - core}, device_id_type=MESH)

    loads[0].wait()
    for load in train_loads:
        load.start()
    for r in range(own):
        row = query_v[r].astype(F32)
        for t in range(groups):
            wide[r, pl.ds(t, layers, stride=groups), :] = row[:, t * LANES:(t + 1) * LANES]

    def query_copy(i):
        return pltpu.make_async_remote_copy(
            src_ref=slabs.at[i],
            dst_ref=arrived.at[i],
            send_sem=q_send.at[i],
            recv_sem=q_recv.at[i],
            device_id={"layer": lax.rem(me + 2 * i + core, layers)},
            device_id_type=MESH,
        )

    def slab_of(i):
        target = lax.rem(me + 2 * i + core, layers)
        start = pl.multiple_of(target * groups, groups)
        return stack([wide[r, pl.ds(start, groups), :] for r in range(own)], axis=1).astype(BF16)

    for i in range(slots):
        slabs[i] = slab_of(i)
        if i == 0:
            pl.semaphore_wait(barrier, layers)

            @pl.when(core == 0)
            def _():
                arrived[0] = slabs[0]

            @pl.when(core != 0)
            def _():
                query_copy(0).start()
        else:
            query_copy(i).start()

    loads[1].wait()
    loads[2].wait()
    left = left_weights(left_v[0])
    right = right_weights(right_v[0])
    low = iota((groups, LANES), 1) < LANES // 2

    def cond_copy(j):
        place = core * chunks + j
        return pltpu.make_async_remote_copy(
            src_ref=cond.at[place],
            dst_ref=cond.at[place],
            send_sem=c_send.at[j],
            recv_sem=c_recv.at[j],
            device_id={"ex": 1 - core},
            device_id_type=MESH,
        )

    for j in range(chunks):
        pieces = []
        for i in range(j * per_chunk, (j + 1) * per_chunk):
            if i == 0:
                @pl.when(core != 0)
                def _():
                    query_copy(0).wait_recv()
            else:
                query_copy(i).wait_recv()
            slab = arrived[i].astype(F32)
            for r in range(own):
                piece = slab[:, r * LANES:(r + 1) * LANES]
                pieces.append(stack([piece, pltpu.roll(piece, LANES // 2, 1)], axis=0))
        both = dot(left, stack(pieces, axis=1).astype(BF16))
        mixed = stack(
            [
                jnp.where(low, both[:groups, n * LANES:(n + 1) * LANES], both[groups:, n * LANES:(n + 1) * LANES])
                for n in range(CHUNK)
            ],
            axis=0,
        ).astype(BF16)
        plain[...] = dot(mixed, right)
        place = core * chunks + j
        for t in range(groups):
            cond[place, :, t * LANES:(t + 1) * LANES] = plain[pl.ds(t, CHUNK, stride=groups), :].astype(BF16)
        cond_copy(j).start()

    for j in range(chunks):
        pltpu.make_async_remote_copy(
            src_ref=cond.at[(1 - core) * chunks + j],
            dst_ref=cond.at[(1 - core) * chunks + j],
            send_sem=c_send.at[j],
            recv_sem=c_recv.at[j],
            device_id={"ex": 1 - core},
            device_id_type=MESH,
        ).wait_recv()

    def rows_of(k):
        return (k % 2) * (rows_all // 2) + (k // 2) * own

    queries = cond[...].reshape(rows_all, groups * LANES)
    total = jnp.zeros((rows_all, LANES), F32)
    for t in range(groups):
        piece = queries[:, t * LANES:(t + 1) * LANES].astype(F32)
        total = total + piece * piece
    norms = jnp.broadcast_to(jnp.sum(total, axis=1, keepdims=True), (rows_all, LANES))

    def norm_copy(k):
        return pltpu.make_async_remote_copy(
            src_ref=norm_sent.at[k],
            dst_ref=norm_got.at[k],
            send_sem=n_send.at[k],
            recv_sem=n_recv.at[k],
            device_id={"layer": lax.rem(me + layers - k, layers)},
            device_id_type=MESH,
        )

    def score_copy(b, k):
        return pltpu.make_async_remote_copy(
            src_ref=sent.at[b, k],
            dst_ref=got.at[b, k],
            send_sem=s_send.at[b, k],
            recv_sem=s_recv.at[b, k],
            device_id={"layer": lax.rem(me + layers - k, layers)},
            device_id_type=MESH,
        )

    for k in range(layers):
        value = norms[rows_of(k):rows_of(k) + own]
        norm_sent[k] = stack([value] * max(1, 8 // own), axis=0)
        if k:
            norm_copy(k).start()

    for b in range(BLOCKS):
        train_loads[b].wait()
        scores[b] = dot_nt(cond[...].reshape(rows_all, groups * LANES), train_v[b])
        for k in range(1, layers):
            value = scores[b, pl.ds(rows_of(k), own), :]
            parts = [value[:, f * width:(f + 1) * width] for f in range(fold)]
            if own * fold < slab_rows:
                parts.append(jnp.zeros((slab_rows - own * fold, width), F32))
            sent[b, k] = stack(parts, axis=0).astype(BF16)
            score_copy(b, k).start()

    norm = norm_sent[0]
    for k in range(1, layers):
        norm_copy(k).wait_recv()
        norm = norm + norm_got[k]
    scale = jnp.sqrt(norm[:own, :1] + epsilon)
    for b in range(BLOCKS):
        summed = jnp.zeros((slab_rows, width), F32)
        for k in range(1, layers):
            score_copy(b, k).wait_recv()
            summed = summed + got[b, k].astype(F32)
        flat = stack([summed[f * own:(f + 1) * own] for f in range(fold)], axis=1)
        out_ref[:, b * block:(b + 1) * block] = (flat + scores[b, pl.ds(0, own), :]) / scale

    for i in range(slots):
        if i == 0:
            @pl.when(core != 0)
            def _():
                query_copy(0).wait_send()
        else:
            query_copy(i).wait_send()
    for j in range(chunks):
        cond_copy(j).wait_send()
    for k in range(1, layers):
        norm_copy(k).wait_send()
        for b in range(BLOCKS):
            score_copy(b, k).wait_send()


def per_device(layers, query_grads, inv_in, inv_out, train_grads):
    own, _, length = query_grads.shape
    examples = train_grads.shape[1]
    groups = length // LANES
    slots = layers // 2
    per_chunk = CHUNK // own
    rows_all = own * layers
    chunks = rows_all // 2 // CHUNK
    block = examples // BLOCKS
    fold = math.gcd(max(1, CHUNK // own), block // LANES)
    width = block // fold
    slab_rows = max(CHUNK, own * fold)
    norm_rows = max(8, own)
    dims = (groups, slots, per_chunk, chunks, rows_all, block, fold, width, slab_rows)
    any_space = pl.BlockSpec(memory_space=pltpu.HBM)
    in_vmem = pl.BlockSpec(memory_space=pltpu.VMEM)
    dma = pltpu.SemaphoreType.DMA
    return pl.pallas_call(
        lambda *refs: kernel(layers, own, dims, *refs),
        out_shape=jax.ShapeDtypeStruct((own, examples), F32),
        in_specs=[any_space] * 4,
        out_specs=in_vmem,
        scratch_shapes=[
            pltpu.VMEM(query_grads.shape, BF16),
            pltpu.VMEM(inv_in.shape, BF16),
            pltpu.VMEM(inv_out.shape, BF16),
            pltpu.VMEM((BLOCKS, block, length), BF16),
            pltpu.VMEM((own, layers * groups, LANES), F32),
            pltpu.VMEM((slots, groups, own * LANES), BF16),
            pltpu.VMEM((slots, groups, own * LANES), BF16),
            pltpu.VMEM((CHUNK * groups, LANES), F32),
            pltpu.VMEM((2 * chunks, CHUNK, length), BF16),
            pltpu.VMEM((BLOCKS, rows_all, block), F32),
            pltpu.VMEM((BLOCKS, layers, slab_rows, width), BF16),
            pltpu.VMEM((BLOCKS, layers, slab_rows, width), BF16),
            pltpu.VMEM((layers, norm_rows, LANES), F32),
            pltpu.VMEM((layers, norm_rows, LANES), F32),
            dma((3,)),
            dma((BLOCKS,)),
            dma((slots,)),
            dma((slots,)),
            dma((chunks,)),
            dma((chunks,)),
            dma((BLOCKS, layers)),
            dma((BLOCKS, layers)),
            dma((layers,)),
            dma((layers,)),
        ],
        compiler_params=pltpu.CompilerParams(
            collective_id=0, has_side_effects=True, vmem_limit_bytes=60 * 1024 * 1024
        ),
        cost_estimate=pl.CostEstimate(
            flops=2 * rows_all * examples * length, bytes_accessed=2 * examples * length, transcendentals=0
        ),
    )(query_grads, inv_in, inv_out, train_grads[0])


def solution(mesh):
    layers = mesh.shape["layer"]
    return jax.shard_map(
        lambda *args: per_device(layers, *args),
        mesh=mesh,
        in_specs=(
            P(("groups", "layer"), None, None),
            P("layer", None, None),
            P("layer", None, None),
            P("layer", ("groups", "ex"), None),
        ),
        out_specs=P("layer", ("groups", "ex")),
        check_vma=False,
    )
```

time: 112 us -> 26 us (0.23)
  blocking collectives: 41.2 us -> 0 us
  waiting for transfers between devices: 40.9 us -> 0 us
  Pallas kernels: 0 us -> 24.4 us
  between operations: 13.4 us -> 0.01 us
  matrix products: 11.2 us -> 0 us
  local copies, waits for them, and re-layouts: 3.29 us -> 1.42 us
  other arithmetic: 1.58 us -> 0 us
    reduce_scatter x1 -> x0, waiting for transfers between devices: 40.9 us -> none  [per_device(): lax.psum_scatter((conditioned, lax.dot_general(conditioned, resident, (((...]
    pallas_call x0 -> x1, Pallas kernels: none -> 24.4 us  [per_device(): pl.pallas_call(lambda *refs: kernel(layers, own, dims, *refs), out_shape=...]
    all_to_all x1 -> x0, blocking collectives: 21.6 us -> none  [per_device(): lax.all_to_all(query_grads, 'layer', split_axis=1, concat_axis=0, tiled=T...]
    psum x1 -> x0, blocking collectives: 19.6 us -> none  [per_device(): totals = lax.psum(square_sum(conditioned, (1,)), 'layer')]
    dot_general x2 -> x0, matrix products: 11.2 us -> none  [the longest x1 9.24 us: per_device(): lax.dot_general(conditioned, resident, (((1,), (1,)), ((), ())), preferre...]
    another operation x2 -> x0, local copies, waits for them, and re-layouts: 1.94 us -> none
    div x1 -> x0, other arithmetic: 1.49 us -> none  [per_device(): return reduced / jnp.sqrt(own_norm + epsilon)[:, None]]
  transfers between devices with their start and end apart: 1 -> 0, of which waited for: 1 -> 0; matrix products, arithmetic and copies ran while one was open for 0% -> 0% of each run, Pallas kernels for 0% -> 0%
where the time goes in v1:
time: 26 us; the launch traced here: 25.8 us
  Pallas kernels  24.4 us (94%)
  local copies, waits for them, and re-layouts  1.42 us (5%)
    pallas_call x1, Pallas kernels, per_device(): pl.pallas_call(lambda *refs: kernel(layers, own, dims, *refs), out_shape=...  24.4 us
    unnamed x1, local copies, waits for them, and re-layouts  1.42 us

profile of v1, /device:TPU:0, one launch (start us, length us, event | category | flops | bytes accessed | tf_op | source)
XLA Modules:
  0.0 25.8 jit_solution(16323255878605718452)
XLA Ops:
  0.0 24.4 %shard_map.46 = f32[8,1536]{1,0:T(8,128)} custom-call(bf16[8,8,4096]{2,1,0:T(8,128)(2,1)} %refs_0_.1, bf16[1,64,64]{2,1,0:T(8,128)(2,1)} %refs_1_.1, bf16[1,64,64]{2,1,0:T(8,128)(2,1)} %refs_2_.1, bf16[1536,4096]{1,0:T(8,128)(2,1)} %bitcast.1), custom_call_target="tpu_custom_call" | custom-call | flops 805306368 | bytes 12582912 | tf_op jit(solution)/shard_map/pallas_call | solution.py:271
  24.4 1.4 %copy.6 = f32[8,1536]{1,0:T(8,128)} copy(f32[8,1536]{1,0:T(8,128)} %shard_map.46) | data formatting | bytes 98304

commit v2 on v1

--- a/solution.py
+++ b/solution.py
@@ -10,7 +10,7 @@
 epsilon = 1e-06
 LANES = 128
 CHUNK = 16
-BLOCKS = 2
+BLOCKS = 3
 MESH = pl.DeviceIdType.MESH
 F32 = jnp.float32
 BF16 = jnp.bfloat16
@@ -58,8 +58,8 @@
     layers, own, dims,
     query_hbm, left_hbm, right_hbm, train_hbm,
     out_ref,
-    query_v, left_v, right_v, train_v, wide, slabs, arrived, plain, cond, scores, sent, got, norm_sent, norm_got,
-    local_sem, train_sem, q_send, q_recv, c_send, c_recv, s_send, s_recv, n_send, n_recv,
+    query_v, left_v, right_v, train_v, wide, slabs, arrived, plain, cond, scores, sent, got, norm_high, norm_low,
+    local_sem, train_sem, q_send, q_recv, c_send, c_recv, s_send, s_recv,
 ):
     groups, slots, per_chunk, chunks, rows_all, block, fold, width, slab_rows = dims
     me = lax.axis_index("layer")
@@ -179,62 +179,19 @@
     def rows_of(k):
         return (k % 2) * (rows_all // 2) + (k // 2) * own
 
-    queries = cond[...].reshape(rows_all, groups * LANES)
-    total = jnp.zeros((rows_all, LANES), F32)
-    for t in range(groups):
-        piece = queries[:, t * LANES:(t + 1) * LANES].astype(F32)
-        total = total + piece * piece
-    norms = jnp.broadcast_to(jnp.sum(total, axis=1, keepdims=True), (rows_all, LANES))
-
-    def norm_copy(k):
+    def score_copy(b, k):
         return pltpu.make_async_remote_copy(
-            src_ref=norm_sent.at[k],
-            dst_ref=norm_got.at[k],
-            send_sem=n_send.at[k],
-            recv_sem=n_recv.at[k],
+            src_ref=sent.at[b, k, :, pl.ds(0, width + LANES if b == 0 else width)],
+            dst_ref=got.at[b, k, :, pl.ds(0, width + LANES if b == 0 else width)],
+            send_sem=s_send.at[b],
+            recv_sem=s_recv.at[b],
             device_id={"layer": lax.rem(me + layers - k, layers)},
             device_id_type=MESH,
         )
 
-    def score_copy(b, k):
-        return pltpu.make_async_remote_copy(
-            src_ref=sent.at[b, k],
-            dst_ref=got.at[b, k],
-            send_sem=s_send.at[b, k],
-            recv_sem=s_recv.at[b, k],
-            device_id={"layer": lax.rem(me + layers - k, layers)},
-            device_id_type=MESH,
-        )
-
-    for k in range(layers):
-        value = norms[rows_of(k):rows_of(k) + own]
-        norm_sent[k] = stack([value] * max(1, 8 // own), axis=0)
-        if k:
-            norm_copy(k).start()
-
-    for b in range(BLOCKS):
-        train_loads[b].wait()
-        scores[b] = dot_nt(cond[...].reshape(rows_all, groups * LANES), train_v[b])
-        for k in range(1, layers):
-            value = scores[b, pl.ds(rows_of(k), own), :]
-            parts = [value[:, f * width:(f + 1) * width] for f in range(fold)]
-            if own * fold < slab_rows:
-                parts.append(jnp.zeros((slab_rows - own * fold, width), F32))
-            sent[b, k] = stack(parts, axis=0).astype(BF16)
-            score_copy(b, k).start()
-
-    norm = norm_sent[0]
-    for k in range(1, layers):
-        norm_copy(k).wait_recv()
-        norm = norm + norm_got[k]
-    scale = jnp.sqrt(norm[:own, :1] + epsilon)
-    for b in range(BLOCKS):
-        summed = jnp.zeros((slab_rows, width), F32)
-        for k in range(1, layers):
-            score_copy(b, k).wait_recv()
-            summed = summed + got[b, k].astype(F32)
-        flat = stack([summed[f * own:(f + 1) * own] for f in range(fold)], axis=1)
-        out_ref[:, b * block:(b + 1) * block] = (flat + scores[b, pl.ds(0, own), :]) / scale
+    def wait_all(buffer, b, sem):
+        others = buffer.at[b, pl.ds(1, layers - 1), :, pl.ds(0, width + LANES if b == 0 else width)]
+        pltpu.make_async_copy(others, others, sem.at[b]).wait()
 
     for i in range(slots):
         if i == 0:
@@ -243,12 +200,50 @@
                 query_copy(0).wait_send()
         else:
             query_copy(i).wait_send()
+
+    for b in range(BLOCKS):
+        train_loads[b].wait()
+        queries = cond[...].reshape(rows_all, groups * LANES)
+        scores[b] = dot_nt(queries, train_v[b])
+        if b == 0:
+            total = jnp.zeros((rows_all, LANES), F32)
+            for t in range(groups):
+                piece = queries[:, t * LANES:(t + 1) * LANES].astype(F32)
+                total = total + piece * piece
+            norms = jnp.broadcast_to(jnp.sum(total, axis=1, keepdims=True), (rows_all, LANES))
+            high = norms.astype(BF16).astype(F32)
+            norm_high[...] = high
+            norm_low[...] = norms - high
+        for k in range(1, layers):
+            rows = pl.ds(rows_of(k), own)
+            value = scores[b, rows, :]
+            parts = [value[:, f * width:(f + 1) * width] for f in range(fold)]
+            if own * fold < slab_rows:
+                parts.append(jnp.zeros((slab_rows - own * fold, width), F32))
+            sent[b, k, :, :width] = stack(parts, axis=0).astype(BF16)
+            if b == 0:
+                parts = [norm_high[rows, :], norm_low[rows, :]]
+                if own * 2 < slab_rows:
+                    parts.append(jnp.zeros((slab_rows - own * 2, LANES), F32))
+                sent[b, k, :, width:] = stack(parts, axis=0).astype(BF16)
+            score_copy(b, k).start()
+
     for j in range(chunks):
         cond_copy(j).wait_send()
-    for k in range(1, layers):
-        norm_copy(k).wait_send()
-        for b in range(BLOCKS):
-            score_copy(b, k).wait_send()
+    for b in range(BLOCKS):
+        wait_all(got, b, s_recv)
+        if b == 0:
+            pair = jnp.zeros((slab_rows, LANES), F32)
+            for k in range(1, layers):
+                pair = pair + got[0, k, :, width:].astype(F32)
+            norm = norm_high[:own] + norm_low[:own] + pair[:own] + pair[own:2 * own]
+            scale = jnp.sqrt(norm[:, :1] + epsilon)
+        summed = jnp.zeros((slab_rows, width), F32)
+        for k in range(1, layers):
+            summed = summed + got[b, k, :, :width].astype(F32)
+        flat = stack([summed[f * own:(f + 1) * own] for f in range(fold)], axis=1)
+        out_ref[:, b * block:(b + 1) * block] = (flat + scores[b, pl.ds(0, own), :]) / scale
+        wait_all(sent, b, s_send)
 
 
 def per_device(layers, query_grads, inv_in, inv_out, train_grads):
@@ -262,8 +257,7 @@
     block = examples // BLOCKS
     fold = math.gcd(max(1, CHUNK // own), block // LANES)
     width = block // fold
-    slab_rows = max(CHUNK, own * fold)
-    norm_rows = max(8, own)
+    slab_rows = max(CHUNK, own * fold, own * 2)
     dims = (groups, slots, per_chunk, chunks, rows_all, block, fold, width, slab_rows)
     any_space = pl.BlockSpec(memory_space=pltpu.HBM)
     in_vmem = pl.BlockSpec(memory_space=pltpu.VMEM)
@@ -284,20 +278,18 @@
             pltpu.VMEM((CHUNK * groups, LANES), F32),
             pltpu.VMEM((2 * chunks, CHUNK, length), BF16),
             pltpu.VMEM((BLOCKS, rows_all, block), F32),
-            pltpu.VMEM((BLOCKS, layers, slab_rows, width), BF16),
-            pltpu.VMEM((BLOCKS, layers, slab_rows, width), BF16),
-            pltpu.VMEM((layers, norm_rows, LANES), F32),
-            pltpu.VMEM((layers, norm_rows, LANES), F32),
+            pltpu.VMEM((BLOCKS, layers, slab_rows, width + LANES), BF16),
+            pltpu.VMEM((BLOCKS, layers, slab_rows, width + LANES), BF16),
+            pltpu.VMEM((rows_all, LANES), F32),
+            pltpu.VMEM((rows_all, LANES), F32),
             dma((3,)),
             dma((BLOCKS,)),
             dma((slots,)),
             dma((slots,)),
             dma((chunks,)),
             dma((chunks,)),
-            dma((BLOCKS, layers)),
-            dma((BLOCKS, layers)),
-            dma((layers,)),
-            dma((layers,)),
+            dma((BLOCKS,)),
+            dma((BLOCKS,)),
         ],
         compiler_params=pltpu.CompilerParams(
             collective_id=0, has_side_effects=True, vmem_limit_bytes=60 * 1024 * 1024

time: 26 us -> 24.3 us (0.935)
  Pallas kernels: 24.4 us -> 22.6 us
    pallas_call x1, Pallas kernels: 24.4 us -> 22.6 us  [per_device(): pl.pallas_call(lambda *refs: kernel(layers, own, dims, *refs), out_shape=...]
where the time goes in v2:
time: 24.3 us; the launch traced here: 24.1 us
  Pallas kernels  22.6 us (93%)
  local copies, waits for them, and re-layouts  1.42 us (6%)
    pallas_call x1, Pallas kernels, per_device(): pl.pallas_call(lambda *refs: kernel(layers, own, dims, *refs), out_shape=...  22.6 us
    unnamed x1, local copies, waits for them, and re-layouts  1.42 us

profile of v2, /device:TPU:0, one launch (start us, length us, event | category | flops | bytes accessed | tf_op | source)
XLA Modules:
  0.0 24.1 jit_solution(5695253494285539507)
XLA Ops:
  0.0 22.6 %shard_map.46 = f32[8,1536]{1,0:T(8,128)} custom-call(bf16[8,8,4096]{2,1,0:T(8,128)(2,1)} %refs_0_.1, bf16[1,64,64]{2,1,0:T(8,128)(2,1)} %refs_1_.1, bf16[1,64,64]{2,1,0:T(8,128)(2,1)} %refs_2_.1, bf16[1536,4096]{1,0:T(8,128)(2,1)} %bitcast.1), custom_call_target="tpu_custom_call" | custom-call | flops 805306368 | bytes 12582912 | tf_op jit(solution)/shard_map/pallas_call | solution.py:265
  22.6 1.4 %copy.6 = f32[8,1536]{1,0:T(8,128)} copy(f32[8,1536]{1,0:T(8,128)} %shard_map.46) | data formatting | bytes 98304

commit v3 on v2

--- a/solution.py
+++ b/solution.py
@@ -65,6 +65,12 @@
     me = lax.axis_index("layer")
     core = lax.axis_index("ex")
 
+    def wrapped(index):
+        return jnp.where(index >= layers, index - layers, index)
+
+    ahead = [wrapped(me + k) for k in range(layers)]
+    behind = [wrapped(me + layers - k) for k in range(layers)]
+
     loads = [
         pltpu.make_async_copy(query_hbm, query_v, local_sem.at[0]),
         pltpu.make_async_copy(left_hbm, left_v, local_sem.at[1]),
@@ -80,7 +86,7 @@
     barrier = pltpu.get_barrier_semaphore()
     for k in range(1, layers):
         pl.semaphore_signal(
-            barrier, inc=1, device_id={"layer": lax.rem(me + k, layers)}, device_id_type=MESH
+            barrier, inc=1, device_id={"layer": ahead[k]}, device_id_type=MESH
         )
     pl.semaphore_signal(barrier, inc=1, device_id={"ex": 1 - core}, device_id_type=MESH)
 
@@ -98,12 +104,12 @@
             dst_ref=arrived.at[i],
             send_sem=q_send.at[i],
             recv_sem=q_recv.at[i],
-            device_id={"layer": lax.rem(me + 2 * i + core, layers)},
+            device_id={"layer": wrapped(me + 2 * i + core)},
             device_id_type=MESH,
         )
 
     def slab_of(i):
-        target = lax.rem(me + 2 * i + core, layers)
+        target = wrapped(me + 2 * i + core)
         start = pl.multiple_of(target * groups, groups)
         return stack([wide[r, pl.ds(start, groups), :] for r in range(own)], axis=1).astype(BF16)
 
@@ -185,7 +191,7 @@
             dst_ref=got.at[b, k, :, pl.ds(0, width + LANES if b == 0 else width)],
             send_sem=s_send.at[b],
             recv_sem=s_recv.at[b],
-            device_id={"layer": lax.rem(me + layers - k, layers)},
+            device_id={"layer": behind[k]},
             device_id_type=MESH,
         )
 
@@ -292,7 +298,7 @@
             dma((BLOCKS,)),
         ],
         compiler_params=pltpu.CompilerParams(
-            collective_id=0, has_side_effects=True, vmem_limit_bytes=60 * 1024 * 1024
+            collective_id=0, has_side_effects=True, vmem_limit_bytes=56 * 1024 * 1024
         ),
         cost_estimate=pl.CostEstimate(
             flops=2 * rows_all * examples * length, bytes_accessed=2 * examples * length, transcendentals=0

time: 24.3 us -> 24.3 us (level)
  no operation moved by 1% of the time
where the time goes in v3:
time: 24.3 us; the launch traced here: 24.1 us
  Pallas kernels  22.6 us (93%)
  local copies, waits for them, and re-layouts  1.42 us (6%)
    pallas_call x1, Pallas kernels, per_device(): pl.pallas_call(lambda *refs: kernel(layers, own, dims, *refs), out_shape=...  22.6 us
    unnamed x1, local copies, waits for them, and re-layouts  1.42 us

profile of v3, /device:TPU:0, one launch (start us, length us, event | category | flops | bytes accessed | tf_op | source)
XLA Modules:
  0.0 24.1 jit_solution(17663853770639985139)
XLA Ops:
  0.0 22.6 %shard_map.46 = f32[8,1536]{1,0:T(8,128)} custom-call(bf16[8,8,4096]{2,1,0:T(8,128)(2,1)} %refs_0_.1, bf16[1,64,64]{2,1,0:T(8,128)(2,1)} %refs_1_.1, bf16[1,64,64]{2,1,0:T(8,128)(2,1)} %refs_2_.1, bf16[1536,4096]{1,0:T(8,128)(2,1)} %bitcast.1), custom_call_target="tpu_custom_call" | custom-call | flops 805306368 | bytes 12582912 | tf_op jit(solution)/shard_map/pallas_call | solution.py:271
  22.6 1.4 %copy.6 = f32[8,1536]{1,0:T(8,128)} copy(f32[8,1536]{1,0:T(8,128)} %shard_map.46) | data formatting | bytes 98304
